TPU v7x, 32 devices: a whole 2x2x4 slice. The times are simulated.
32 devices in a mesh: seq: 4 (over y, x), rep: 8 (over z, core).
Axes of the slice: x: 2, y: 2, z: 4, core: 2. Of those that a mesh axis runs over, the one named last changes fastest.
Arguments:
- mixer_in: bfloat16 [8, 512, 4096], P('rep', 'seq'), may hold values from -6 to 6
- write_proj: bfloat16 [8, 512, 512], P('rep', 'seq'), may hold values from -6 to 6
- read_proj: bfloat16 [8, 512, 512], P('rep', 'seq'), may hold values from -0.5 to 0.5
- dt_steps: int32 [8, 512, 64], P('rep', 'seq'), may hold values from 1 to 16
- decay_exp: int32 [8, 512, 64], P('rep', 'seq'), may hold values from 1 to 50000, as said below
- norm_gain: float32 [4096], P('seq'), may hold values from 0.1 to 1.9
- skip_gain: float32 [64], P('seq'), may hold values from 1 to 4
- out_grad: bfloat16 [8, 512, 4096], P('rep', 'seq'), may hold values from -80 to 80
Outputs:
- mixer_grad: bfloat16 [8, 512, 4096], P('rep', 'seq')
- read_grad: bfloat16 [8, 512, 512], P('rep', 'seq')
- gain_grad: float32 [4096], P('seq')
- skip_grad: float32 [64], P('seq')
Inputs may be any that keep to these rules, and one draw needn't show every extreme that they name: The decay factor of head h at position t is exp(-decay_exp / 65536).
All inputs are finite; a program needn't handle non-finite values.
Results may differ from a plain program's by a relative error of at most 0.015.
Values may be sent and summed in bfloat16 or wider, within the bound.
A program may use at most 64 MiB of HBM per device.

v0:
```python
import jax
import jax.numpy as jnp
from jax import lax
from jax.sharding import PartitionSpec as P

H = 64
P_SIZE = 64
N = 128
G = 4
HG = 16


def entering(array, axis, combine, identity, reverse):
    devices, here = (lax.axis_size(axis), lax.axis_index(axis))
    everything = jax.tree.map(lambda part: lax.all_gather(part, axis), array)
    start = jax.tree.map(
        lambda part, zero: jnp.broadcast_to(jnp.asarray(zero, part.dtype), part.shape),
        array,
        identity,
    )

    def lap(k, before):
        at = devices - 1 - k if reverse else k
        reached = at > here if reverse else at < here
        new = combine(before, jax.tree.map(lambda part: part[at], everything))
        return jax.tree.map(lambda a, b: jnp.where(reached, a, b), new, before)

    return lax.fori_loop(0, devices, lap, start)


def contract(form, left, right):
    return jnp.einsum(form, left, right, preferred_element_type=jnp.float32)


def decay_weights(log_decay, step_size):
    length = log_decay.shape[2]
    causal = jnp.arange(length)[:, None] >= jnp.arange(length)[None, :]
    spread = jnp.where(causal, log_decay[:, :, :, None] - log_decay[:, :, None, :], 0.0)
    return jnp.where(causal, jnp.exp(spread), 0.0) * step_size[:, :, None, :]


def block_front(mixed, write, read, steps, decay):
    length = mixed.shape[3]
    log_decay = -(
        jnp.cumsum(jnp.transpose(decay).reshape(G, HG, length), axis=2).astype(jnp.float32)
        / 65536.0
    )
    step_size = jnp.transpose(steps).reshape(G, HG, length).astype(jnp.float32) / 16.0
    weights = decay_weights(log_decay, step_size)
    scores = contract("gnt,gns->gts", read, write)
    mixing = (scores[:, None] * weights).astype(jnp.bfloat16)
    inner_part = contract("gjts,gjps->gjpt", mixing, mixed)
    ending = jnp.exp(log_decay[:, :, -1:] - log_decay) * step_size
    weighted = (mixed.astype(jnp.float32) * ending[:, :, None, :]).astype(jnp.bfloat16)
    span_state = contract("gjps,gns->gjpn", weighted, write).astype(jnp.bfloat16)
    block_decay = jnp.exp(log_decay[:, :, -1]).astype(jnp.bfloat16)
    readout = jnp.exp(log_decay)
    return (log_decay, step_size, mixing, inner_part, ending, span_state, block_decay, readout)


def block_middle(mixed, read, skip_full, gain_full, upstream, inner_part, readout, carried):
    mixed_wide = mixed.astype(jnp.float32)
    mixer_out = (
        inner_part
        + readout[:, :, None, :] * contract("gnt,gjpn->gjpt", read, carried)
        + skip_full[:, :, None, None] * mixed_wide
    )
    inverse = lax.rsqrt(jnp.mean(mixer_out * mixer_out, axis=(1, 2), keepdims=True) + 1e-05)
    normed = mixer_out * inverse
    upstream_wide = upstream.astype(jnp.float32)
    normed_grad = upstream_wide * gain_full[:, :, :, None]
    gain_part = jnp.sum(upstream_wide * normed, axis=3)
    delta_wide = inverse * (
        normed_grad - normed * jnp.mean(normed_grad * normed, axis=(1, 2), keepdims=True)
    )
    skip_part = jnp.sum(delta_wide * mixed_wide, axis=(2, 3))
    delta_half = delta_wide.astype(jnp.bfloat16)
    scaled_delta = (delta_wide * readout[:, :, None, :]).astype(jnp.bfloat16)
    state_grad = contract("gjpt,gnt->gjpn", scaled_delta, read).astype(jnp.bfloat16)
    read_part = contract("gjpt,gjpn->gnt", scaled_delta, carried)
    return (delta_wide, delta_half, state_grad, read_part, gain_part, skip_part)


def block_back(
    mixed,
    write,
    skip_full,
    log_decay,
    step_size,
    mixing,
    ending,
    delta_wide,
    delta_half,
    read_part,
    carried_grad,
):
    weights = decay_weights(log_decay, step_size)
    mix_grad = contract("gjpt,gjps->gjts", delta_half, mixed)
    score_grad = jnp.sum(mix_grad * weights, axis=1).astype(jnp.bfloat16)
    read_grad = contract("gts,gns->gnt", score_grad, write) + read_part
    mixer_grad = contract("gjts,gjpt->gjps", mixing, delta_half)
    mixer_grad = mixer_grad + ending[:, :, None, :] * contract(
        "gns,gjpn->gjps", write, carried_grad
    )
    mixer_grad = mixer_grad + skip_full[:, :, None, None] * delta_wide
    return (mixer_grad.astype(jnp.bfloat16), read_grad.astype(jnp.bfloat16))


def forward_join(earlier, later):
    decay_early, state_early = earlier
    decay_late, state_late = later
    joined = (decay_early.astype(jnp.float32) * decay_late.astype(jnp.float32)).astype(jnp.bfloat16)
    state = (
        decay_late.astype(jnp.float32)[..., None, None] * state_early.astype(jnp.float32)
        + state_late.astype(jnp.float32)
    ).astype(jnp.bfloat16)
    return (joined, state)


def backward_join(earlier, later):
    decay_early, grad_early = earlier
    decay_late, grad_late = later
    joined = (decay_early.astype(jnp.float32) * decay_late.astype(jnp.float32)).astype(jnp.bfloat16)
    grads = (
        grad_late.astype(jnp.float32)
        + decay_late.astype(jnp.float32)[..., None, None] * grad_early.astype(jnp.float32)
    ).astype(jnp.bfloat16)
    return (joined, grads)


def neutral(block_decay, span_state):
    return (jnp.ones(block_decay.shape, jnp.bfloat16), jnp.zeros(span_state.shape, jnp.bfloat16))


def states_whole(block_decay, span_state):
    return entering(
        (block_decay, span_state), "seq", forward_join, neutral(block_decay, span_state), False
    )[1]


def grads_whole(block_decay, state_grad):
    return entering(
        (block_decay, state_grad), "seq", backward_join, neutral(block_decay, state_grad), True
    )[1]


def on_device(mixer_in, write_proj, read_proj, dt_steps, decay_exp, norm_gain, skip_gain, out_grad):
    length = mixer_in.shape[1]
    mixed = jnp.transpose(mixer_in[0].reshape(length, G, HG, P_SIZE), (1, 2, 3, 0))
    upstream = jnp.transpose(out_grad[0].reshape(length, G, HG, P_SIZE), (1, 2, 3, 0))
    write = jnp.transpose(write_proj[0].reshape(length, G, N), (1, 2, 0))
    read = jnp.transpose(read_proj[0].reshape(length, G, N), (1, 2, 0))
    gain_whole, skip_whole = (
        lax.all_gather(norm_gain, "seq", axis=0, tiled=True),
        lax.all_gather(skip_gain, "seq", axis=0, tiled=True),
    )
    gain_full = gain_whole.reshape(G, HG, P_SIZE)
    skip_full = skip_whole.reshape(G, HG)
    log_decay, step_size, mixing, inner_part, ending, span_state, block_decay, readout = (
        block_front(mixed, write, read, dt_steps[0], decay_exp[0])
    )
    carried = states_whole(block_decay, span_state)
    delta_wide, delta_half, state_grad, read_part, gain_part, skip_part = block_middle(
        mixed, read, skip_full, gain_full, upstream, inner_part, readout, carried
    )
    carried_grad = grads_whole(block_decay, state_grad)
    mixer_grad, read_grad = block_back(
        mixed,
        write,
        skip_full,
        log_decay,
        step_size,
        mixing,
        ending,
        delta_wide,
        delta_half,
        read_part,
        carried_grad,
    )
    gain_flat = gain_part.reshape(H * P_SIZE)
    skip_flat = skip_part.reshape(H)
    gain_share, skip_share = (
        lax.psum_scatter(gain_flat, "seq", scatter_dimension=0, tiled=True),
        lax.psum_scatter(skip_flat, "seq", scatter_dimension=0, tiled=True),
    )
    gain_piece, skip_piece = lax.psum((gain_share, skip_share), "rep")
    mixer_rows = jnp.transpose(mixer_grad, (3, 0, 1, 2)).reshape(1, length, H * P_SIZE)
    read_rows = jnp.transpose(read_grad, (2, 0, 1)).reshape(1, length, G * N)
    return (mixer_rows, read_rows, gain_piece, skip_piece)


def solution(mesh):
    in_specs = (
        P("rep", "seq", None),
        P("rep", "seq", None),
        P("rep", "seq", None),
        P("rep", "seq", None),
        P("rep", "seq", None),
        P("seq"),
        P("seq"),
        P("rep", "seq", None),
    )
    out_specs = (P("rep", "seq", None), P("rep", "seq", None), P("seq"), P("seq"))
    return jax.shard_map(
        on_device, mesh=mesh, in_specs=in_specs, out_specs=out_specs, check_vma=False
    )
```

profile of v0, /device:TPU:0, one launch (start us, length us, event | category | flops | bytes accessed | tf_op | source)
XLA Modules:
  0.0 163.8 jit_solution(3676155176131560743)
XLA Ops:
  8.0 2.2 %reduce_window_sum.11 = s32[4,16,128]{2,1,0:T(8,128)S(1)} reduce-window(s32[4,16,128]{2,1,0:T(8,128)} %bitcast.151, s32[]{:T(128)} %constant.82.clone.1), window={size=1x1x128 pad=0_0x0_0x127_0}, to_apply=%region_0.0 | reduce-window | flops 1040384 | bytes 65540 | tf_op jit(solution)/shard_map/jit(cumsum)/reduce_window_sum | solution.py:45
  17.4 11.3 %all-reduce = f32[64]{0:T(128)S(1)} all-reduce(f32[64]{0:T(128)S(1)} %dynamic-update-slice), channel_id=1, replica_groups=mesh['seq'=4,'rep'=8] {'seq'}, use_global_device_ids=true, to_apply=%add | all-reduce | flops 64 | bytes 512
  28.9 7.4 %all_gather.28 = f32[4096]{0:T(1024)S(1)} all-gather(f32[1024]{0:T(1024)S(1)} %copy-done.17), channel_id=1, replica_groups=mesh['seq'=4,'rep'=8] {'seq'}, dimensions={0}, use_global_device_ids=true | all-gather | bytes 20480 | tf_op jit(solution)/shard_map/all_gather | solution.py:154
  36.5 8.0 %all-gather = bf16[16,16,1]{1,2,0:T(2,128)(2,1)S(1)} all-gather(bf16[4,16,1]{1,2,0:T(2,128)(2,1)S(1)} %copy.61), channel_id=2, replica_groups=mesh['seq'=4,'rep'=8] {'seq'}, dimensions={0}, use_global_device_ids=true | all-gather | bytes 640 | tf_op jit(solution)/shard_map/all_gather | solution.py:15
  44.6 2.7 %copy.64 = f32[1,128,4096]{1,2,0:T(8,128)} copy(bf16[1,128,4096]{2,1,0:T(8,128)(2,1)} %param.19) | data formatting | bytes 3145728 | tf_op jit(solution)/shard_map/convert_element_type | solution.py:70
  47.5 3.4 %fusion.18 = f32[4,16,128,64]{2,3,1,0:T(8,128)} fusion(bf16[4,16,64,128]{3,2,1,0:T(8,128)(2,1)S(1)} %bitcast.129, f32[4,16,128]{2,1,0:T(8,128)S(1)} %bitcast.147, f32[4,16,128]{2,1,0:T(8,128)S(1)} %copy.57, f32[4,128,128]{2,1,0:T(8,128)S(1)} %fusion.32, pred[128,128]{1,0:T(8,128)(4,1)S(1)} %iota_compare_fusion), kind=kOutput, calls=%fused_computation.36 | convolution fusion | flops 140509184 | bytes 3489792 | tf_op jit(solution)/shard_map/gjts,gjps->gjpt/dot_general | solution.py:32
  50.9 20.5 %all-gather.6.cloned.1.call-done = bf16[16,16,64,128]{3,2,1,0:T(8,128)(2,1)} async-done(((bf16[4,16,64,128]{3,2,1,0:T(8,128)(2,1)}), bf16[16,16,64,128]{3,2,1,0:T(8,128)(2,1)}) %all-gather.6.cloned.1.call-update) | async-done | bytes 4194320 | tf_op jit(solution)/shard_map/all_gather | solution.py:15
  71.4 8.1 %while.30 = (s32[]{:T(128)}, bf16[4,16,64,128]{3,2,1,0:T(8,128)(2,1)S(1)}, s32[]{:T(128)}, bf16[4,4,16]{2,1,0:T(4,128)(2,1)S(1)}, bf16[4,4,16,64,128]{4,3,2,1,0:T(8,128)(2,1)}, /*index=5*/s32[]{:T(128)}, s32[]{:T(128)}) while((s32[]{:T(128)}, bf16[4,16,64,128]{3,2,1,0:T(8,128)(2,1)S(1)}, s32[]{:T(128)}, ...), condition=%wide.region_2.3_spmd.clone, body=%wide.region_1.2_spmd.clone.sunk | while | flops 3670084 | bytes 3146481 | solution.py:28
  73.5 2.0 %fusion.48 = bf16[4,16,64,128]{3,2,1,0:T(8,128)(2,1)S(1)} fusion(bf16[4,16,64,128]{3,2,1,0:T(8,128)(2,1)S(1)} %get-tuple-element.400, bf16[4,4,16,64,128]{4,3,2,1,0:T(8,128)(2,1)} %get-tuple-element.410, s32[]{:T(128)S(6)} %copy.79, f32[4,16]{1,0:T(4,128)S(1)} %bitcast_convert_fusion.4, pred[]{:T(512)S(6)} %compare.6, pred[]{:T(512)S(6)} %lt.44), kind=kLoop, calls=%fused_computation.2.clone.1 | loop fusion | flops 3670016 | bytes 3145990 | tf_op jit(solution)/shard_map/while/body/eval_jaxpr/jit(_where)/select_n | solution.py:26
  75.5 2.0 %fusion.48 = bf16[4,16,64,128]{3,2,1,0:T(8,128)(2,1)S(1)} fusion(bf16[4,16,64,128]{3,2,1,0:T(8,128)(2,1)S(1)} %get-tuple-element.400, bf16[4,4,16,64,128]{4,3,2,1,0:T(8,128)(2,1)} %get-tuple-element.410, s32[]{:T(128)S(6)} %copy.79, f32[4,16]{1,0:T(4,128)S(1)} %bitcast_convert_fusion.4, pred[]{:T(512)S(6)} %compare.6, pred[]{:T(512)S(6)} %lt.44), kind=kLoop, calls=%fused_computation.2.clone.1 | loop fusion | flops 3670016 | bytes 3145990 | tf_op jit(solution)/shard_map/while/body/eval_jaxpr/jit(_where)/select_n | solution.py:26
  79.6 3.7 %multiply_reduce_fusion.3 = (f32[4,128]{1,0:T(4,128)S(1)}, f32[4,16,64,128]{3,2,1,0:T(8,128)S(1)}, f32[4,16,64,128]{3,2,1,0:T(8,128)}) fusion(bf16[4,16,64,128]{3,2,1,0:T(8,128)(2,1)S(1)} %bitcast.130, f32[4,16]{1,0:T(4,128)S(1)} %mul.212, f32[4,16,128]{2,1,0:T(8,128)S(1)} %copy.60, f32[4,16,128,64]{2,3,1,0:T(8,128)} %fusion.18, ...), kind=kOutput, calls=%fused_computation.34 | convolution fusion | flops 137887232 | bytes 8554752 | tf_op jit(solution)/shard_map/gnt,gjpn->gjpt/dot_general | solution.py:32
  85.2 2.0 %fusion.6 = (f32[4,16]{1,0:T(4,128)}, f32[4,16,64,128]{3,2,1,0:T(8,128)S(1)}) fusion(bf16[4,16,64,128]{3,2,1,0:T(8,128)(2,1)S(1)} %bitcast.131, f32[4,128]{1,0:T(4,128)S(1)} %get-tuple-element.326, f32[4,16,64,128]{3,2,1,0:T(8,128)S(1)} %get-tuple-element.317, f32[4,16,64,128]{3,2,1,0:T(8,128)S(1)} %bitcast.127, f32[4,16,64]{2,1,0:T(8,128)S(1)} %mul.217, ...), kind=kLoop, calls=%fused_computation.16 | loop fusion | flops 4194240 | bytes 7360768 | tf_op jit(solution)/shard_map/reduce_sum | solution.py:76
  95.2 2.4 %convolution_bitcast_fusion.1 = f32[128,4,128]{0,2,1:T(8,128)S(1)} fusion(bf16[4,16,64,128]{3,2,1,0:T(8,128)(2,1)S(1)} %get-tuple-element.230, f32[4,16,64,128]{3,2,1,0:T(8,128)} %copy-done.1, f32[4,16,128]{2,1,0:T(8,128)} %copy-done.3), kind=kOutput, calls=%fused_computation.41 | convolution fusion | flops 135266304 | bytes 3440640 | tf_op jit(solution)/shard_map/gjpt,gjpn->gnt/dot_general | solution.py:32
  97.9 2.2 %multiply_reduce_fusion = bf16[4,128,128]{2,1,0:T(8,128)(2,1)S(1)} fusion(bf16[4,16,64,128]{3,2,1,0:T(8,128)(2,1)S(1)} %bitcast.132, f32[4,16,128]{2,1,0:T(8,128)S(1)} %bitcast.148, f32[4,16,128]{2,1,0:T(8,128)S(1)} %copy-done.14, pred[128,128]{1,0:T(8,128)(4,1)S(1)} %copy-done.16, f32[4,16,64,128]{3,2,1,0:T(8,128)S(1)} %copy-done.2), kind=kOutput, calls=%fused_computation.8 | convolution fusion | flops 140967936 | bytes 3358720 | tf_op jit(solution)/shard_map/gjpt,gjps->gjts/dot_general | solution.py:32
  101.1 15.6 %all-reduce.4 = (f32[4096]{0:T(1024)S(1)}, f32[64]{0:T(128)S(1)}) all-reduce(f32[4096]{0:T(1024)S(1)} %reshape.119, f32[64]{0:T(128)S(1)} %reshape.120), channel_id=5, replica_groups=mesh['seq'=4,'rep'=8] {'seq'}, use_global_device_ids=true, to_apply=%region_9.10.clone | all-reduce | flops 4160 | bytes 33280
  116.8 14.4 %all-reduce.3 = (f32[1024]{0:T(1024)}, f32[16]{0:T(128)}) all-reduce(f32[1024]{0:T(1024)S(1)} %dynamic-slice.2, f32[16]{0:T(128)S(1)} %dynamic-slice.4), channel_id=1, replica_groups=mesh['seq'=4,'rep'=8] {'rep'}, use_global_device_ids=true, to_apply=%region_10.11 | all-reduce | flops 1040 | bytes 8320 | tf_op jit(solution)/shard_map/psum | solution.py:186
  131.2 3.9 %fusion.17 = f32[4,16,64,128]{3,2,1,0:T(8,128)} fusion(f32[4,16,128]{2,1,0:T(8,128)S(1)} %bitcast.149, f32[4,16,128]{2,1,0:T(8,128)S(1)} %copy-done.14, f32[4,128,128]{2,1,0:T(8,128)S(1)} %copy-done.7, pred[128,128]{1,0:T(8,128)(4,1)S(1)} %copy-done.16, f32[4,16,64,128]{3,2,1,0:T(8,128)} %copy-done.1), kind=kOutput, calls=%fused_computation.35 | convolution fusion | flops 141033472 | bytes 4538368 | tf_op jit(solution)/shard_map/gjts,gjpt->gjps/dot_general | solution.py:32
  135.1 8.2 %all-gather.8.cloned.1.call-done = bf16[16,16,64,128]{3,2,1,0:T(8,128)(2,1)} async-done(((bf16[4,16,64,128]{3,2,1,0:T(8,128)(2,1)}), bf16[16,16,64,128]{3,2,1,0:T(8,128)(2,1)}) %all-gather.8.cloned.1.call-update) | async-done | bytes 4194320 | tf_op jit(solution)/shard_map/all_gather | solution.py:15
  143.3 8.2 %while.31 = (s32[]{:T(128)}, bf16[4,16,64,128]{3,2,1,0:T(8,128)(2,1)S(1)}, s32[]{:T(128)}, bf16[4,4,16,64,128]{4,3,2,1,0:T(8,128)(2,1)}, bf16[4,4,16]{2,1,0:T(4,...) while((s32[]{:T(128)}, bf16[4,16,64,128]{3,2,1,0:T(8,128)(2,1)S(1)}, s32[]{:T(128)}, ...), condition=%wide.region_6.7_spmd.clone, body=%wide.region_5.6_spmd.clone.sunk | while | flops 3670088 | bytes 3146543 | solution.py:28
  143.3 2.0 %fusion.49 = bf16[4,16,64,128]{3,2,1,0:T(8,128)(2,1)S(1)} fusion(bf16[4,16,64,128]{3,2,1,0:T(8,128)(2,1)S(1)} %get-tuple-element.423, f32[4,16]{1,0:T(4,128)S(1)} %bitcast_convert_fusion.5, bf16[4,4,16,64,128]{4,3,2,1,0:T(8,128)(2,1)} %get-tuple-element.434, s32[]{:T(128)S(6)} %select_n.96, pred[]{:T(512)S(6)} %compare.7, pred[]{:T(512)S(6)} %gt.12), kind=kLoop, calls=%fused_computation.6.clone.1 | loop fusion | flops 3670016 | bytes 3145990 | tf_op jit(solution)/shard_map/while/body/eval_jaxpr/jit(_where)/select_n | solution.py:26
  145.4 2.0 %fusion.49 = bf16[4,16,64,128]{3,2,1,0:T(8,128)(2,1)S(1)} fusion(bf16[4,16,64,128]{3,2,1,0:T(8,128)(2,1)S(1)} %get-tuple-element.423, f32[4,16]{1,0:T(4,128)S(1)} %bitcast_convert_fusion.5, bf16[4,4,16,64,128]{4,3,2,1,0:T(8,128)(2,1)} %get-tuple-element.434, s32[]{:T(128)S(6)} %select_n.96, pred[]{:T(512)S(6)} %compare.7, pred[]{:T(512)S(6)} %gt.12), kind=kLoop, calls=%fused_computation.6.clone.1 | loop fusion | flops 3670016 | bytes 3145990 | tf_op jit(solution)/shard_map/while/body/eval_jaxpr/jit(_where)/select_n | solution.py:26
  147.4 2.0 %fusion.49 = bf16[4,16,64,128]{3,2,1,0:T(8,128)(2,1)S(1)} fusion(bf16[4,16,64,128]{3,2,1,0:T(8,128)(2,1)S(1)} %get-tuple-element.423, f32[4,16]{1,0:T(4,128)S(1)} %bitcast_convert_fusion.5, bf16[4,4,16,64,128]{4,3,2,1,0:T(8,128)(2,1)} %get-tuple-element.434, s32[]{:T(128)S(6)} %select_n.96, pred[]{:T(512)S(6)} %compare.7, pred[]{:T(512)S(6)} %gt.12), kind=kLoop, calls=%fused_computation.6.clone.1 | loop fusion | flops 3670016 | bytes 3145990 | tf_op jit(solution)/shard_map/while/body/eval_jaxpr/jit(_where)/select_n | solution.py:26
  149.5 2.0 %fusion.49 = bf16[4,16,64,128]{3,2,1,0:T(8,128)(2,1)S(1)} fusion(bf16[4,16,64,128]{3,2,1,0:T(8,128)(2,1)S(1)} %get-tuple-element.423, f32[4,16]{1,0:T(4,128)S(1)} %bitcast_convert_fusion.5, bf16[4,4,16,64,128]{4,3,2,1,0:T(8,128)(2,1)} %get-tuple-element.434, s32[]{:T(128)S(6)} %select_n.96, pred[]{:T(512)S(6)} %compare.7, pred[]{:T(512)S(6)} %gt.12), kind=kLoop, calls=%fused_computation.6.clone.1 | loop fusion | flops 3670016 | bytes 3145990 | tf_op jit(solution)/shard_map/while/body/eval_jaxpr/jit(_where)/select_n | solution.py:26
  151.6 4.0 %fusion.15 = bf16[128,4,16,64]{0,3,2,1:T(8,128)(2,1)S(1)} fusion(f32[4,16,64,128]{3,2,1,0:T(8,128)} %get-tuple-element.329, f32[4,16,128,64]{2,3,1,0:T(8,128)} %fusion.18, f32[4,16,64,128]{3,2,1,0:T(8,128)} %fusion.17, bf16[128,4,16,64]{0,3,2,1:T(8,128)(2,1)S(1)} %bitcast.133, f32[128,4,16,64]{0,3,2,1:T(8,128)} %bitcast.125, ...), kind=kOutput, calls=%fused_computation.26 | convolution fusion | flops 142082048 | bytes 11751680 | tf_op jit(solution)/shard_map/gns,gjpn->gjps/dot_general | solution.py:32
  (92 shorter events, 23.1 us)
Async XLA Ops:
  7.2 64.3 %all-gather.6.cloned.1.call-start = ((), (), s32[]{:S(2)}) async-start(), calls=%async_computation | async-start | bytes 5242880 | tf_op jit(solution)/shard_map/all_gather | solution.py:15
  8.0 39.5 %copy-start.10 = (f32[1,128,64]{1,2,0:T(8,128)}, f32[1,128,64]{1,2,0:T(8,128)S(1)}, u32[]{:S(2)}) copy-start(f32[1,128,64]{1,2,0:T(8,128)S(1)} %convert_multiply_fusion.3) | copy-start | bytes 98308
  14.3 1.7 %copy-start.18 = (u32[32]{0:T(128)S(1)}, u32[32]{0:T(128)}, u32[]{:S(2)}) copy-start(u32[32]{0:T(128)} %constant.98) | copy-start | bytes 388
  14.3 2.9 %copy-start.19 = (f32[16]{0:T(128)S(1)}, f32[16]{0:T(128)}, u32[]{:S(2)}) copy-start(f32[16]{0:T(128)} %param.18) | copy-start | bytes 196
  14.3 14.6 %copy-start.17 = (f32[1024]{0:T(1024)S(1)}, f32[1024]{0:T(1024)}, u32[]{:S(2)}) copy-start(f32[1024]{0:T(1024)} %param.17) | copy-start | bytes 12292
  14.3 22.0 %copy-start.12 = (bf16[1,128,512]{2,1,0:T(8,128)(2,1)S(1)}, bf16[1,128,512]{2,1,0:T(8,128)(2,1)}, u32[]{:S(2)}) copy-start(bf16[1,128,512]{2,1,0:T(8,128)(2,1)} %param.14) | copy-start | bytes 393220
  15.8 127.5 %all-gather.8.cloned.1.call-start = ((), (), s32[]{:S(2)}) async-start(), calls=%async_computation.1 | async-start | bytes 5242880 | tf_op jit(solution)/shard_map/all_gather | solution.py:15
  15.9 31.6 %copy-start.13 = (f32[4,16,128]{2,1,0:T(8,128)}, f32[4,16,128]{2,1,0:T(8,128)S(1)}, u32[]{:S(2)}) copy-start(f32[4,16,128]{2,1,0:T(8,128)S(1)} %copy.57) | copy-start | bytes 98308
  36.3 48.9 %copy-start.4 = (f32[4,16,64]{2,1,0:T(8,128)}, f32[4,16,64]{2,1,0:T(8,128)S(1)}, u32[]{:S(2)}) copy-start(f32[4,16,64]{2,1,0:T(8,128)S(1)} %mul.217) | copy-start | bytes 49156
  44.6 42.6 %copy-start.3 = (f32[4,16,128]{2,1,0:T(8,128)}, f32[4,16,128]{2,1,0:T(8,128)S(1)}, u32[]{:S(2)}) copy-start(f32[4,16,128]{2,1,0:T(8,128)S(1)} %copy.60) | copy-start | bytes 98308
  47.3 3.6 %copy-start.15 = (pred[128,128]{1,0:T(8,128)(4,1)}, pred[128,128]{1,0:T(8,128)(4,1)S(1)}, u32[]{:S(2)}) copy-start(pred[128,128]{1,0:T(8,128)(4,1)S(1)} %iota_compare_fusion) | copy-start | bytes 49156
  47.5 3.4 %copy-start.6 = (f32[4,128,128]{2,1,0:T(8,128)}, f32[4,128,128]{2,1,0:T(8,128)S(1)}, u32[]{:S(2)}) copy-start(f32[4,128,128]{2,1,0:T(8,128)S(1)} %fusion.32) | copy-start | bytes 786436
  79.5 3.7 %copy-start = (f32[1,128,4096]{1,2,0:T(8,128)S(1)}, f32[1,128,4096]{1,2,0:T(8,128)}, u32[]{:S(2)}) copy-start(f32[1,128,4096]{1,2,0:T(8,128)} %copy.64) | copy-start | bytes 6291460
  87.2 1.3 copy-start.1
  93.6 4.1 %copy-start.11 = (f32[1,128,64]{1,2,0:T(8,128)S(1)}, f32[1,128,64]{1,2,0:T(8,128)}, u32[]{:S(2)}) copy-start(f32[1,128,64]{1,2,0:T(8,128)} %copy-done.10) | copy-start | bytes 98308
  93.6 4.1 %copy-start.14 = (f32[4,16,128]{2,1,0:T(8,128)S(1)}, f32[4,16,128]{2,1,0:T(8,128)}, u32[]{:S(2)}) copy-start(f32[4,16,128]{2,1,0:T(8,128)} %copy-done.13) | copy-start | bytes 98308
  93.6 4.1 %copy-start.16 = (pred[128,128]{1,0:T(8,128)(4,1)S(1)}, pred[128,128]{1,0:T(8,128)(4,1)}, u32[]{:S(2)}) copy-start(pred[128,128]{1,0:T(8,128)(4,1)} %copy-done.15) | copy-start | bytes 49156
  95.2 2.6 %copy-start.2 = (f32[4,16,64,128]{3,2,1,0:T(8,128)S(1)}, f32[4,16,64,128]{3,2,1,0:T(8,128)}, u32[]{:S(2)}) copy-start(f32[4,16,64,128]{3,2,1,0:T(8,128)} %copy-done.1) | copy-start | bytes 6291460
  97.9 33.4 %copy-start.7 = (f32[4,128,128]{2,1,0:T(8,128)S(1)}, f32[4,128,128]{2,1,0:T(8,128)}, u32[]{:S(2)}) copy-start(f32[4,128,128]{2,1,0:T(8,128)} %copy-done.6) | copy-start | bytes 786436
  143.3 8.3 %copy-start.5 = (f32[4,16,64]{2,1,0:T(8,128)S(1)}, f32[4,16,64]{2,1,0:T(8,128)}, u32[]{:S(2)}) copy-start(f32[4,16,64]{2,1,0:T(8,128)} %copy-done.4) | copy-start | bytes 49156
  143.3 8.3 %copy-start.8 = (f32[128,4,16]{0,2,1:T(8,128)S(1)}, f32[128,4,16]{0,2,1:T(8,128)}, u32[]{:S(2)}) copy-start(f32[128,4,16]{0,2,1:T(8,128)} %copy.66) | copy-start | bytes 98308
  143.3 8.3 %copy-start.9 = (f32[128,4,16]{0,2,1:T(8,128)S(1)}, f32[128,4,16]{0,2,1:T(8,128)}, u32[]{:S(2)}) copy-start(f32[128,4,16]{0,2,1:T(8,128)} %copy.65) | copy-start | bytes 98308
Sparse Core Ops, SparseCore 0:
  15.9 55.5 all-gather.5
  90.1 53.1 all-gather.7
where the time goes:
time: 165 us; the launch traced here: 164 us
  blocking collectives  56.8 us (34%)
  waiting for transfers between devices  28.7 us (17%)
  other arithmetic  24 us (15%)
  matrix products  22.9 us (14%)
  between operations  16.3 us (10%)
  local copies, waits for them, and re-layouts  14.7 us (9%)
    all_gather x2, waiting for transfers between devices, entering(): everything = jax.tree.map(lambda part: lax.all_gather(part, axis), array)  28.7 us
    unnamed x2, blocking collectives  27 us
    dot_general x10, matrix products, contract(): return jnp.einsum(form, left, right, preferred_element_type=jnp.float32)  22.9 us
    select_n x8, other arithmetic, lap(): return jax.tree.map(lambda a, b: jnp.where(reached, a, b), new, before)  16.1 us
    psum x1, blocking collectives, on_device(): gain_piece, skip_piece = lax.psum((gain_share, skip_share), 'rep')  14.4 us
    all_gather x1, blocking collectives, entering(): everything = jax.tree.map(lambda part: lax.all_gather(part, axis), array)  8.02 us
    all_gather x1, blocking collectives, on_device(): lax.all_gather(norm_gain, 'seq', axis=0, tiled=True)  7.41 us
    unnamed x49, local copies, waits for them, and re-layouts  6.17 us
  transfers between devices with their start and end apart: 2, of which 2 were waited for; matrix products, arithmetic and copies ran while one was open for 13% of the time, Pallas kernels for 0%

commit v1 on v0

--- a/solution.py
+++ b/solution.py
@@ -1,7 +1,14 @@
+import functools
+
 import jax
 import jax.numpy as jnp
 from jax import lax
+from jax.experimental import pallas as pl
+from jax.experimental.pallas import tpu as pltpu
 from jax.sharding import PartitionSpec as P
+
+MESH = pl.DeviceIdType.MESH
+F32, BF16 = jnp.float32, jnp.bfloat16
 
 H = 64
 P_SIZE = 64
@@ -41,10 +48,9 @@
 
 def block_front(mixed, write, read, steps, decay):
     length = mixed.shape[3]
-    log_decay = -(
-        jnp.cumsum(jnp.transpose(decay).reshape(G, HG, length), axis=2).astype(jnp.float32)
-        / 65536.0
-    )
+    exponents = jnp.transpose(decay).reshape(G, HG, 1, length)
+    upto = jnp.arange(length)[:, None] >= jnp.arange(length)[None, :]
+    log_decay = -(jnp.sum(jnp.where(upto, exponents, 0), axis=3).astype(jnp.float32) / 65536.0)
     step_size = jnp.transpose(steps).reshape(G, HG, length).astype(jnp.float32) / 16.0
     weights = decay_weights(log_decay, step_size)
     scores = contract("gnt,gns->gts", read, write)
@@ -189,7 +195,408 @@
     return (mixer_rows, read_rows, gain_piece, skip_piece)
 
 
+def mm(a, b, dims):
+    return lax.dot_general(a, b, (dims, ((), ())), preferred_element_type=F32)
+
+
+NN, NT, TN = ((1,), (0,)), ((1,), (1,)), ((0,), (0,))
+
+
+def grouped_kernel(
+    n,
+    reps,
+    x_ref,
+    b_ref,
+    c_ref,
+    u_ref,
+    steps_ref,
+    decay_ref,
+    gain_ref,
+    skip_ref,
+    out_ref,
+    read_ref,
+    sums_ref,
+    xs,
+    us,
+    bs,
+    cs,
+    table_out,
+    table,
+    cols,
+    ends,
+    mix,
+    weights,
+    y,
+    half,
+    inv,
+    carried,
+    carried_grad,
+    read_part,
+    grad_out,
+    read_out,
+    sums,
+    send_sem,
+    recv_sem,
+    local_sem,
+    rep_send,
+    rep_recv,
+):
+    me, my_rep = lax.axis_index("seq"), lax.axis_index("rep")
+    length, width, state = xs.shape[1], xs.shape[2], bs.shape[2]
+    heads = table.shape[1] // 2
+    pairs = width // (2 * P_SIZE)
+    lanes = 2 * P_SIZE
+    peers = [lax.rem(me + d, n) for d in range(1, n)]
+    rep_peers = [lax.rem(my_rep + d, reps) for d in range(1, reps)]
+
+    barrier = pltpu.get_barrier_semaphore()
+    for peer in peers:
+        pl.semaphore_signal(barrier, inc=1, device_id={"seq": peer}, device_id_type=MESH)
+    for peer in rep_peers:
+        pl.semaphore_signal(barrier, inc=1, device_id={"rep": peer}, device_id_type=MESH)
+
+    row = lax.broadcasted_iota(jnp.int32, (length, length), 0)
+    col = lax.broadcasted_iota(jnp.int32, (length, length), 1)
+    causal = row >= col
+    left = lax.broadcasted_iota(jnp.int32, (length, lanes), 1) < P_SIZE
+    left_row = lax.broadcasted_iota(jnp.int32, (1, lanes), 1) < P_SIZE
+
+    triangle = jnp.where(causal, 1.0, 0.0).astype(BF16)
+    decay = decay_ref[...]
+    high = (decay >> 8).astype(F32).astype(BF16)
+    low = (decay & 255).astype(F32).astype(BF16)
+    total = mm(triangle, high, NN) * 256.0 + mm(triangle, low, NN)
+    both = jnp.concatenate([total * (-1.0 / 65536.0), steps_ref[...].astype(F32) / 16.0], axis=1)
+    flipped = both.T
+    for g in range(n):
+        table_out[g, :heads] = flipped[g * heads : (g + 1) * heads]
+        table_out[g, heads:] = flipped[(n + g) * heads : (n + g + 1) * heads]
+
+    def part(ref, g, size):
+        return ref.at[:, pl.ds(pl.multiple_of(g * size, size), size)]
+
+    def source(a, g):
+        if a == 0:
+            return table_out.at[g]
+        return part((x_ref, b_ref, c_ref, u_ref)[a - 1], g, (width, state, state, width)[a - 1])
+
+    target = (table, xs, bs, cs, us)
+
+    def send(a, d):
+        return pltpu.make_async_remote_copy(
+            src_ref=source(a, peers[d]),
+            dst_ref=target[a].at[me],
+            send_sem=send_sem.at[a, d],
+            recv_sem=recv_sem.at[a, me],
+            device_id={"seq": peers[d]},
+            device_id_type=MESH,
+        )
+
+    def arrival(a, d):
+        return pltpu.make_async_remote_copy(
+            src_ref=source(a, peers[d]),
+            dst_ref=target[a].at[peers[d]],
+            send_sem=send_sem.at[a, d],
+            recv_sem=recv_sem.at[a, peers[d]],
+            device_id={"seq": peers[d]},
+            device_id_type=MESH,
+        )
+
+    own = [
+        pltpu.make_async_copy(source(a, me), target[a].at[me], local_sem.at[a]) for a in range(5)
+    ]
+    for copy in own:
+        copy.start()
+    pl.semaphore_wait(barrier, n - 1 + reps - 1)
+    for a in range(4):
+        for d in range(n - 1):
+            send(a, d).start()
+    for copy in own:
+        copy.wait()
+    for a in range(4):
+        for d in range(n - 1):
+            arrival(a, d).wait_recv()
+    for d in range(n - 1):
+        send(4, d).start()
+
+    def span(j):
+        return slice(j * lanes, (j + 1) * lanes)
+
+    def pick(values, j):
+        return jnp.where(left, values[:, 2 * j : 2 * j + 1], values[:, 2 * j + 1 : 2 * j + 2])
+
+    def pick_row(values, j):
+        return jnp.where(left_row, values[:, 2 * j : 2 * j + 1], values[:, 2 * j + 1 : 2 * j + 2])
+
+    def skip_pair(j):
+        return jnp.where(left_row, skip_ref[2 * j], skip_ref[2 * j + 1])
+
+    def apart(values):
+        zero = jnp.zeros_like(values)
+        return jnp.concatenate([jnp.where(left, values, zero), jnp.where(left, zero, values)], axis=0)
+
+    def closing(k):
+        return jnp.exp(cols[k][length - 1 :, :]).astype(BF16).astype(F32)
+
+    carried[0] = jnp.zeros(carried.shape[1:], BF16)
+    carried_grad[n] = jnp.zeros(carried_grad.shape[1:], BF16)
+
+    def forward(k, _):
+        tab = table[k]
+        copies = length // (2 * heads)
+        c = jnp.concatenate([tab] * copies, axis=0).T
+        swapped = jnp.concatenate([tab[heads:], tab[:heads]] * copies, axis=0).T
+        cols[k] = c
+        ending = jnp.exp(c[length - 1 :, :] - c) * swapped
+        ends[k] = ending
+        readout = jnp.exp(c)
+        block_decay = closing(k)
+        write, read = bs[k], cs[k]
+        scores = mm(read, write, NT)
+        squares = jnp.zeros((length, lanes), F32)
+        for j in range(pairs):
+            mixed = []
+            for e in range(2):
+                h = 2 * j + e
+                spread = jnp.where(causal, c[:, h : h + 1] - tab[h : h + 1, :], -1e30)
+                w = jnp.exp(spread) * tab[heads + h : heads + h + 1, :]
+                weights[k, j, :, e * length : (e + 1) * length] = w
+                mixed.append((scores * w).astype(BF16))
+            mixing = jnp.concatenate(mixed, axis=1)
+            mix[k, j] = mixing
+            x = xs[k, :, span(j)]
+            wide = x.astype(F32)
+            before = carried[k, :, span(j)]
+            out = mm(mixing, apart(x), NN)
+            out = out + pick(readout, j) * mm(read, before, NN) + skip_pair(j) * wide
+            y[k, :, span(j)] = out
+            squares = squares + out * out
+            weighted = (wide * pick(ending, j)).astype(BF16)
+            grown = mm(write, weighted, TN).astype(BF16).astype(F32)
+            carried[k + 1, :, span(j)] = (
+                pick_row(block_decay, j) * before.astype(F32) + grown
+            ).astype(BF16)
+        mean = jnp.sum(squares, axis=1, keepdims=True) / width
+        inv[k] = jnp.broadcast_to(lax.rsqrt(mean + 1e-05), inv.shape[1:])
+        return 0
+
+    lax.fori_loop(0, n, forward, 0)
+
+    for d in range(n - 1):
+        arrival(4, d).wait_recv()
+    sums[my_rep] = jnp.zeros(sums.shape[1:], F32)
+
+    def middle(i, _):
+        k = n - 1 - i
+        inverse = inv[k]
+        readout = jnp.exp(cols[k])
+        block_decay = closing(k)
+        read = cs[k]
+        inner = jnp.zeros((length, lanes), F32)
+        for j in range(pairs):
+            up = us[k, :, span(j)].astype(F32)
+            normed = y[k, :, span(j)] * inverse
+            product = up * normed
+            inner = inner + product * gain_ref[:, span(j)]
+            sums[my_rep, 0:1, span(j)] += jnp.sum(product, axis=0, keepdims=True)
+        mean = jnp.sum(inner, axis=1, keepdims=True) / width
+        kept = jnp.zeros((length, state), F32)
+        for j in range(pairs):
+            up = us[k, :, span(j)].astype(F32)
+            normed = y[k, :, span(j)] * inverse
+            delta = inverse * (up * gain_ref[:, span(j)] - normed * mean)
+            y[k, :, span(j)] = delta
+            half[k, :, span(j)] = delta.astype(BF16)
+            wide = xs[k, :, span(j)].astype(F32)
+            sums[my_rep, 1:2, span(j)] += jnp.sum(delta * wide, axis=0, keepdims=True)
+            scaled = (delta * pick(readout, j)).astype(BF16)
+            state_grad = mm(read, scaled, TN).astype(BF16).astype(F32)
+            kept = kept + mm(scaled, carried[k, :, span(j)], NT)
+            later = carried_grad[k + 1, :, span(j)].astype(F32)
+            carried_grad[k, :, span(j)] = (
+                state_grad + pick_row(block_decay, j) * later
+            ).astype(BF16)
+        read_part[k] = kept
+        return 0
+
+    lax.fori_loop(0, n, middle, 0)
+
+    def rep_send_copy(d):
+        return pltpu.make_async_remote_copy(
+            src_ref=sums.at[my_rep],
+            dst_ref=sums.at[my_rep],
+            send_sem=rep_send.at[d],
+            recv_sem=rep_recv.at[my_rep],
+            device_id={"rep": rep_peers[d]},
+            device_id_type=MESH,
+        )
+
+    def rep_arrival(d):
+        return pltpu.make_async_remote_copy(
+            src_ref=sums.at[my_rep],
+            dst_ref=sums.at[rep_peers[d]],
+            send_sem=rep_send.at[d],
+            recv_sem=rep_recv.at[rep_peers[d]],
+            device_id={"rep": rep_peers[d]},
+            device_id_type=MESH,
+        )
+
+    for d in range(reps - 1):
+        rep_send_copy(d).start()
+
+    def results(d, k):
+        return [
+            pltpu.make_async_remote_copy(
+                src_ref=values.at[k],
+                dst_ref=part(ref, me, size),
+                send_sem=send_sem.at[a, d],
+                recv_sem=recv_sem.at[a, me],
+                device_id={"seq": k},
+                device_id_type=MESH,
+            )
+            for a, values, ref, size in (
+                (5, grad_out, out_ref, width),
+                (6, read_out, read_ref, state),
+            )
+        ]
+
+    def result_arrivals(d):
+        peer = peers[d]
+        return [
+            pltpu.make_async_remote_copy(
+                src_ref=values.at[peer],
+                dst_ref=part(ref, peer, size),
+                send_sem=send_sem.at[a, d],
+                recv_sem=recv_sem.at[a, peer],
+                device_id={"seq": peer},
+                device_id_type=MESH,
+            )
+            for a, values, ref, size in (
+                (5, grad_out, out_ref, width),
+                (6, read_out, read_ref, state),
+            )
+        ]
+
+    def back(i, _):
+        k = lax.rem(me + 1 + i, n)
+        write = bs[k]
+        ending = ends[k]
+        grads = jnp.zeros((length, length), F32)
+        for j in range(pairs):
+            delta = half[k, :, span(j)]
+            product = mm(delta, apart(xs[k, :, span(j)]), NT) * weights[k, j]
+            grads = grads + product[:, :length] + product[:, length:]
+            turned = mm(mix[k, j], delta, TN)
+            out = jnp.where(left, turned[:length], turned[length:])
+            out = out + pick(ending, j) * mm(write, carried_grad[k + 1, :, span(j)], NN)
+            out = out + skip_pair(j) * y[k, :, span(j)]
+            grad_out[k, :, span(j)] = out.astype(BF16)
+        read_out[k] = (mm(grads.astype(BF16), write, NN) + read_part[k]).astype(BF16)
+
+        @pl.when(i < n - 1)
+        def _():
+            for copy in results(i, k):
+                copy.start()
+
+        return 0
+
+    lax.fori_loop(0, n, back, 0)
+
+    last = [
+        pltpu.make_async_copy(grad_out.at[me], part(out_ref, me, width), local_sem.at[5]),
+        pltpu.make_async_copy(read_out.at[me], part(read_ref, me, state), local_sem.at[6]),
+    ]
+    for copy in last:
+        copy.start()
+    for d in range(reps - 1):
+        rep_arrival(d).wait_recv()
+    everything = sums[0]
+    for r in range(1, reps):
+        everything = everything + sums[r]
+    sums_ref[...] = everything
+    for d in range(n - 1):
+        for a in range(5):
+            send(a, d).wait_send()
+        for copy in results(d, peers[d]):
+            copy.wait_send()
+        for copy in result_arrivals(d):
+            copy.wait_recv()
+    for d in range(reps - 1):
+        rep_send_copy(d).wait_send()
+    for copy in last:
+        copy.wait()
+
+
+def by_groups(n, reps, mixer_in, write_proj, read_proj, dt_steps, decay_exp, norm_gain, skip_gain, out_grad):
+    length, channels = mixer_in.shape[1:]
+    width, state = channels // n, write_proj.shape[2] // n
+    heads = width // P_SIZE
+    pairs = heads // 2
+    hbm = pl.BlockSpec(memory_space=pl.ANY)
+    vmem = pl.BlockSpec(memory_space=pltpu.VMEM)
+    smem = pl.BlockSpec(memory_space=pltpu.SMEM)
+    wide, square = (n, length, width), (n, length, state)
+    mixer_grad, read_grad, sums = pl.pallas_call(
+        functools.partial(grouped_kernel, n, reps),
+        out_shape=(
+            jax.ShapeDtypeStruct((length, channels), BF16),
+            jax.ShapeDtypeStruct((length, n * state), BF16),
+            jax.ShapeDtypeStruct((2, width), F32),
+        ),
+        in_specs=[hbm, hbm, hbm, hbm, vmem, vmem, vmem, smem],
+        out_specs=(hbm, hbm, vmem),
+        scratch_shapes=[
+            pltpu.VMEM(wide, BF16),
+            pltpu.VMEM(wide, BF16),
+            pltpu.VMEM(square, BF16),
+            pltpu.VMEM(square, BF16),
+            pltpu.VMEM((n, 2 * heads, length), F32),
+            pltpu.VMEM((n, 2 * heads, length), F32),
+            pltpu.VMEM((n, length, length), F32),
+            pltpu.VMEM((n, length, length), F32),
+            pltpu.VMEM((n, pairs, length, 2 * length), BF16),
+            pltpu.VMEM((n, pairs, length, 2 * length), F32),
+            pltpu.VMEM(wide, F32),
+            pltpu.VMEM(wide, BF16),
+            pltpu.VMEM((n, length, 2 * P_SIZE), F32),
+            pltpu.VMEM((n + 1, state, width), BF16),
+            pltpu.VMEM((n + 1, state, width), BF16),
+            pltpu.VMEM(square, F32),
+            pltpu.VMEM(wide, BF16),
+            pltpu.VMEM(square, BF16),
+            pltpu.VMEM((reps, 2, width), F32),
+            pltpu.SemaphoreType.DMA((7, n - 1)),
+            pltpu.SemaphoreType.DMA((7, n)),
+            pltpu.SemaphoreType.DMA((7,)),
+            pltpu.SemaphoreType.DMA((max(reps - 1, 1),)),
+            pltpu.SemaphoreType.DMA((reps,)),
+        ],
+        compiler_params=pltpu.CompilerParams(
+            collective_id=0, has_side_effects=True, vmem_limit_bytes=48 * 1024 * 1024
+        ),
+    )(
+        mixer_in[0],
+        write_proj[0],
+        read_proj[0],
+        out_grad[0],
+        dt_steps[0],
+        decay_exp[0],
+        norm_gain.reshape(1, width),
+        skip_gain,
+    )
+    skip_grad = jnp.sum(sums[1].reshape(heads, P_SIZE), axis=1)
+    return (mixer_grad[None], read_grad[None], sums[0], skip_grad)
+
+
 def solution(mesh):
+    n, reps = mesh.shape["seq"], mesh.shape["rep"]
+
+    def step(*args):
+        batch, length = args[0].shape[:2]
+        if n == G and batch == 1 and length == N and 2 * P_SIZE == N:
+            return by_groups(n, reps, *args)
+        return on_device(*args)
+
     in_specs = (
         P("rep", "seq", None),
         P("rep", "seq", None),
@@ -202,5 +609,5 @@
     )
     out_specs = (P("rep", "seq", None), P("rep", "seq", None), P("seq"), P("seq"))
     return jax.shard_map(
-        on_device, mesh=mesh, in_specs=in_specs, out_specs=out_specs, check_vma=False
-    )
+        step, mesh=mesh, in_specs=in_specs, out_specs=out_specs, check_vma=False
+    )

time: 165 us -> 63.4 us (0.38)
  blocking collectives: 56.8 us -> 0 us
  Pallas kernels: 0 us -> 54.5 us
  waiting for transfers between devices: 28.7 us -> 0 us
  other arithmetic: 24 us -> 0.63 us
  matrix products: 22.9 us -> 0 us
  between operations: 16.3 us -> 0.7 us
  local copies, waits for them, and re-layouts: 14.7 us -> 7.3 us
    pallas_call x0 -> x1, Pallas kernels: none -> 54.5 us  [by_groups(): pl.pallas_call(functools.partial(grouped_kernel, n, reps), out_shape=(jax...]
    all_gather x2 -> x0, waiting for transfers between devices: 28.7 us -> none  [entering(): everything = jax.tree.map(lambda part: lax.all_gather(part, axis), array)]
    unnamed x2 -> x0, blocking collectives: 27 us -> none
    dot_general x10 -> x0, matrix products: 22.9 us -> none  [contract(): return jnp.einsum(form, left, right, preferred_element_type=jnp.float32)]
    select_n x8 -> x0, other arithmetic: 16.1 us -> none  [lap(): return jax.tree.map(lambda a, b: jnp.where(reached, a, b), new, before)]
    all_gather x2 -> x0, blocking collectives: 15.4 us -> none  [the longest x1 8.02 us: entering(): everything = jax.tree.map(lambda part: lax.all_gather(part, axis), array)]
    psum x1 -> x0, blocking collectives: 14.4 us -> none  [on_device(): gain_piece, skip_piece = lax.psum((gain_share, skip_share), 'rep')]
    reduce_sum x2 -> x1, other arithmetic: 3.94 us -> 0.63 us  [by_groups(): skip_grad = jnp.sum(sums[1].reshape(heads, P_SIZE), axis=1)]
  transfers between devices with their start and end apart: 2 -> 0, of which waited for: 2 -> 0; matrix products, arithmetic and copies ran while one was open for 13% -> 0% of each run, Pallas kernels for 0% -> 0%
where the time goes in v1:
time: 63.4 us; the launch traced here: 63.1 us
  Pallas kernels  54.5 us (86%)
  local copies, waits for them, and re-layouts  7.3 us (12%)
  between operations  0.7 us (1%)
    pallas_call x1, Pallas kernels, by_groups(): pl.pallas_call(functools.partial(grouped_kernel, n, reps), out_shape=(jax...  54.5 us
    unnamed x18, local copies, waits for them, and re-layouts  6.63 us

profile of v1, /device:TPU:0, one launch (start us, length us, event | category | flops | bytes accessed | tf_op | source)
XLA Modules:
  0.0 63.1 jit_solution(5154474773968253311)
XLA Ops:
  0.6 0.0 copy-start.6
  0.6 0.0 copy-start.2
  0.7 0.9 %copy.12 = s32[1,128,64]{2,1,0:T(8,128)S(1)} copy(s32[1,128,64]{1,2,0:T(8,128)} %param.11) | data formatting | bytes 65536 | tf_op args[3]
  1.5 0.0 copy-done.6
  1.6 0.1 copy.13
  1.6 0.0 copy-start.4
  1.7 0.0 copy-start.5
  1.7 0.0 copy-done.2
  1.7 0.7 %copy-done.4 = f32[1024]{0:T(1024)S(1)} copy-done((f32[1024]{0:T(1024)S(1)}, f32[1024]{0:T(1024)}, u32[]{:S(2)}) %copy-start.4) | copy-done | bytes 4120
  2.3 0.0 copy-done.5
  2.3 0.0 copy-start
  2.3 1.2 %copy-done = bf16[1,128,4096]{2,1,0:T(8,128)(2,1)S(1)} copy-done((bf16[1,128,4096]{2,1,0:T(8,128)(2,1)S(1)}, bf16[1,128,4096]{2,1,0:T(8,128)(2,1)}, u32[]{:S(2)}) %copy-start) | copy-done | bytes 1048600
  3.6 0.0 copy-start.1
  3.6 1.2 %copy-done.1 = bf16[1,128,4096]{2,1,0:T(8,128)(2,1)S(1)} copy-done((bf16[1,128,4096]{2,1,0:T(8,128)(2,1)S(1)}, bf16[1,128,4096]{2,1,0:T(8,128)(2,1)}, u32[]{:S(2)}) %copy-start.1) | copy-done | bytes 1048600
  4.8 0.0 copy-start.3
  4.8 0.9 %copy-done.3 = bf16[1,128,512]{2,1,0:T(8,128)(2,1)S(1)} copy-done((bf16[1,128,512]{2,1,0:T(8,128)(2,1)S(1)}, bf16[1,128,512]{2,1,0:T(8,128)(2,1)}, u32[]{:S(2)}) %copy-start.3) | copy-done | bytes 131096
  5.7 54.5 %shard_map.111 = (bf16[128,4096]{1,0:T(8,128)(2,1)S(1)}, bf16[128,512]{1,0:T(8,128)(2,1)S(1)}, f32[2,1024]{1,0:T(2,128)S(1)}) custom-call(bf16[128,4096]{1,0:T(8,128)(2,1)S(1)} %bitcast.10, bf16[128,512]{1,0:T(8,128)(2,1)S(1)} %bitcast.15, bf16[128,512]{1,0:T(8,128)(2,1)S(1)} %bitcast.16, bf16[128,4096]{1,0:T(8,128)(2,1)S(1)} %bitcast.11, ...), custom_call_target="tpu_custom_call" | custom-call | tf_op jit(solution)/shard_map/pallas_call | solution.py:539
  60.2 0.6 slice_reduce_fusion
  60.8 0.1 reshape_squeeze.3
  60.9 0.6 reduce_sum.9
  61.5 1.0 %copy.16 = bf16[1,128,4096]{2,1,0:T(8,128)(2,1)} copy(bf16[1,128,4096]{2,1,0:T(8,128)(2,1)S(1)} %bitcast.12) | data formatting | bytes 2097152
  62.5 0.7 %copy.17 = bf16[1,128,512]{2,1,0:T(8,128)(2,1)} copy(bf16[1,128,512]{2,1,0:T(8,128)(2,1)S(1)} %bitcast.17) | data formatting | bytes 262144
Async XLA Ops:
  0.6 0.9 %copy-start.6 = (s32[1,128,64]{1,2,0:T(8,128)S(1)}, s32[1,128,64]{1,2,0:T(8,128)}, u32[]{:S(2)}) copy-start(s32[1,128,64]{1,2,0:T(8,128)} %param.12) | copy-start | bytes 98308
  0.6 1.0 %copy-start.2 = (bf16[1,128,512]{2,1,0:T(8,128)(2,1)S(1)}, bf16[1,128,512]{2,1,0:T(8,128)(2,1)}, u32[]{:S(2)}) copy-start(bf16[1,128,512]{2,1,0:T(8,128)(2,1)} %param.9) | copy-start | bytes 393220
  1.6 0.7 %copy-start.4 = (f32[1024]{0:T(1024)S(1)}, f32[1024]{0:T(1024)}, u32[]{:S(2)}) copy-start(f32[1024]{0:T(1024)} %param.13) | copy-start | bytes 12292
  1.7 0.7 %copy-start.5 = (f32[16]{0:T(128)S(1)}, f32[16]{0:T(128)}, u32[]{:S(2)}) copy-start(f32[16]{0:T(128)} %skip_ref.1) | copy-start | bytes 196
  2.3 1.2 %copy-start = (bf16[1,128,4096]{2,1,0:T(8,128)(2,1)S(1)}, bf16[1,128,4096]{2,1,0:T(8,128)(2,1)}, u32[]{:S(2)}) copy-start(bf16[1,128,4096]{2,1,0:T(8,128)(2,1)} %param.8) | copy-start | bytes 3145732
  3.6 1.2 %copy-start.1 = (bf16[1,128,4096]{2,1,0:T(8,128)(2,1)S(1)}, bf16[1,128,4096]{2,1,0:T(8,128)(2,1)}, u32[]{:S(2)}) copy-start(bf16[1,128,4096]{2,1,0:T(8,128)(2,1)} %param.15) | copy-start | bytes 3145732
  4.8 0.9 %copy-start.3 = (bf16[1,128,512]{2,1,0:T(8,128)(2,1)S(1)}, bf16[1,128,512]{2,1,0:T(8,128)(2,1)}, u32[]{:S(2)}) copy-start(bf16[1,128,512]{2,1,0:T(8,128)(2,1)} %param.10) | copy-start | bytes 393220

commit v2 on v1

--- a/solution.py
+++ b/solution.py
@@ -215,7 +215,8 @@
     skip_ref,
     out_ref,
     read_ref,
-    sums_ref,
+    gain_out,
+    skip_out,
     xs,
     us,
     bs,
@@ -246,7 +247,15 @@
     heads = table.shape[1] // 2
     pairs = width // (2 * P_SIZE)
     lanes = 2 * P_SIZE
-    peers = [lax.rem(me + d, n) for d in range(1, n)]
+    swap = lax.rem(my_rep, 2)
+
+    def partner(i):
+        step = lax.rem(i + 1, n)
+        minor, major = lax.rem(step, 2), step // 2
+        minor, major = minor + swap * (major - minor), major + swap * (minor - major)
+        return lax.rem(me + minor, 2) + 2 * lax.rem(me // 2 + major, 2)
+
+    peers = [partner(d) for d in range(n - 1)]
     rep_peers = [lax.rem(my_rep + d, reps) for d in range(1, reps)]
 
     barrier = pltpu.get_barrier_semaphore()
@@ -261,16 +270,15 @@
     left = lax.broadcasted_iota(jnp.int32, (length, lanes), 1) < P_SIZE
     left_row = lax.broadcasted_iota(jnp.int32, (1, lanes), 1) < P_SIZE
 
-    triangle = jnp.where(causal, 1.0, 0.0).astype(BF16)
+    triangle = jnp.where(row <= col, 1.0, 0.0).astype(BF16)
     decay = decay_ref[...]
     high = (decay >> 8).astype(F32).astype(BF16)
     low = (decay & 255).astype(F32).astype(BF16)
-    total = mm(triangle, high, NN) * 256.0 + mm(triangle, low, NN)
-    both = jnp.concatenate([total * (-1.0 / 65536.0), steps_ref[...].astype(F32) / 16.0], axis=1)
-    flipped = both.T
+    total = mm(high, triangle, NN) * 256.0 + mm(low, triangle, NN)
+    log_decay, step_size = total * (-1.0 / 65536.0), steps_ref[...].astype(F32) / 16.0
     for g in range(n):
-        table_out[g, :heads] = flipped[g * heads : (g + 1) * heads]
-        table_out[g, heads:] = flipped[(n + g) * heads : (n + g + 1) * heads]
+        table_out[g, :heads] = log_decay[g * heads : (g + 1) * heads]
+        table_out[g, heads:] = step_size[g * heads : (g + 1) * heads]
 
     def part(ref, g, size):
         return ref.at[:, pl.ds(pl.multiple_of(g * size, size), size)]
@@ -308,16 +316,14 @@
     for copy in own:
         copy.start()
     pl.semaphore_wait(barrier, n - 1 + reps - 1)
-    for a in range(4):
+    for a in (0, 2, 3, 1):
         for d in range(n - 1):
             send(a, d).start()
     for copy in own:
         copy.wait()
-    for a in range(4):
+    for a in (0, 2, 3):
         for d in range(n - 1):
             arrival(a, d).wait_recv()
-    for d in range(n - 1):
-        send(4, d).start()
 
     def span(j):
         return slice(j * lanes, (j + 1) * lanes)
@@ -341,33 +347,41 @@
     carried[0] = jnp.zeros(carried.shape[1:], BF16)
     carried_grad[n] = jnp.zeros(carried_grad.shape[1:], BF16)
 
-    def forward(k, _):
+    def front(k, _):
         tab = table[k]
         copies = length // (2 * heads)
         c = jnp.concatenate([tab] * copies, axis=0).T
         swapped = jnp.concatenate([tab[heads:], tab[:heads]] * copies, axis=0).T
         cols[k] = c
-        ending = jnp.exp(c[length - 1 :, :] - c) * swapped
-        ends[k] = ending
-        readout = jnp.exp(c)
-        block_decay = closing(k)
-        write, read = bs[k], cs[k]
-        scores = mm(read, write, NT)
-        squares = jnp.zeros((length, lanes), F32)
+        ends[k] = jnp.exp(c[length - 1 :, :] - c) * swapped
+        scores = mm(cs[k], bs[k], NT)
         for j in range(pairs):
-            mixed = []
             for e in range(2):
                 h = 2 * j + e
                 spread = jnp.where(causal, c[:, h : h + 1] - tab[h : h + 1, :], -1e30)
                 w = jnp.exp(spread) * tab[heads + h : heads + h + 1, :]
                 weights[k, j, :, e * length : (e + 1) * length] = w
-                mixed.append((scores * w).astype(BF16))
-            mixing = jnp.concatenate(mixed, axis=1)
-            mix[k, j] = mixing
+                mix[k, j, :, e * length : (e + 1) * length] = (scores * w).astype(BF16)
+        return 0
+
+    lax.fori_loop(0, n, front, 0)
+
+    for d in range(n - 1):
+        send(4, d).start()
+    for d in range(n - 1):
+        arrival(1, d).wait_recv()
+
+    def forward(k, _):
+        ending = ends[k]
+        readout = jnp.exp(cols[k])
+        block_decay = closing(k)
+        write, read = bs[k], cs[k]
+        squares = jnp.zeros((length, lanes), F32)
+        for j in range(pairs):
             x = xs[k, :, span(j)]
             wide = x.astype(F32)
             before = carried[k, :, span(j)]
-            out = mm(mixing, apart(x), NN)
+            out = mm(mix[k, j], apart(x), NN)
             out = out + pick(readout, j) * mm(read, before, NN) + skip_pair(j) * wide
             y[k, :, span(j)] = out
             squares = squares + out * out
@@ -478,7 +492,7 @@
         ]
 
     def back(i, _):
-        k = lax.rem(me + 1 + i, n)
+        k = partner(i)
         write = bs[k]
         ending = ends[k]
         grads = jnp.zeros((length, length), F32)
@@ -513,7 +527,16 @@
     everything = sums[0]
     for r in range(1, reps):
         everything = everything + sums[r]
-    sums_ref[...] = everything
+    gain_out[...] = everything[0:1]
+    lane = lax.broadcasted_iota(jnp.int32, (width, lanes), 0)
+    head = lax.broadcasted_iota(jnp.int32, (width, lanes), 1)
+    members = jnp.where(lane // P_SIZE == head, 1.0, 0.0).astype(BF16)
+    rest, skip = everything[1:2], jnp.zeros((1, lanes), F32)
+    for _ in range(3):
+        piece = rest.astype(BF16)
+        skip = skip + mm(piece, members, NN)
+        rest = rest - piece.astype(F32)
+    skip_out[...] = skip
     for d in range(n - 1):
         for a in range(5):
             send(a, d).wait_send()
@@ -532,19 +555,20 @@
     width, state = channels // n, write_proj.shape[2] // n
     heads = width // P_SIZE
     pairs = heads // 2
-    hbm = pl.BlockSpec(memory_space=pl.ANY)
+    hbm = pl.BlockSpec(memory_space=pltpu.HBM)
     vmem = pl.BlockSpec(memory_space=pltpu.VMEM)
     smem = pl.BlockSpec(memory_space=pltpu.SMEM)
     wide, square = (n, length, width), (n, length, state)
-    mixer_grad, read_grad, sums = pl.pallas_call(
+    mixer_grad, read_grad, gain_grad, skip_grad = pl.pallas_call(
         functools.partial(grouped_kernel, n, reps),
         out_shape=(
             jax.ShapeDtypeStruct((length, channels), BF16),
             jax.ShapeDtypeStruct((length, n * state), BF16),
-            jax.ShapeDtypeStruct((2, width), F32),
+            jax.ShapeDtypeStruct((1, width), F32),
+            jax.ShapeDtypeStruct((1, 2 * P_SIZE), F32),
         ),
         in_specs=[hbm, hbm, hbm, hbm, vmem, vmem, vmem, smem],
-        out_specs=(hbm, hbm, vmem),
+        out_specs=(hbm, hbm, vmem, vmem),
         scratch_shapes=[
             pltpu.VMEM(wide, BF16),
             pltpu.VMEM(wide, BF16),
@@ -572,20 +596,19 @@
             pltpu.SemaphoreType.DMA((reps,)),
         ],
         compiler_params=pltpu.CompilerParams(
-            collective_id=0, has_side_effects=True, vmem_limit_bytes=48 * 1024 * 1024
+            collective_id=0, has_side_effects=True, vmem_limit_bytes=62 * 1024 * 1024
         ),
     )(
         mixer_in[0],
         write_proj[0],
         read_proj[0],
         out_grad[0],
-        dt_steps[0],
-        decay_exp[0],
+        dt_steps[0].T,
+        decay_exp[0].T,
         norm_gain.reshape(1, width),
         skip_gain,
     )
-    skip_grad = jnp.sum(sums[1].reshape(heads, P_SIZE), axis=1)
-    return (mixer_grad[None], read_grad[None], sums[0], skip_grad)
+    return (mixer_grad[None], read_grad[None], gain_grad[0], skip_grad[0, :heads])
 
 
 def solution(mesh):

time: 63.4 us -> 60.4 us (0.953)
  local copies, waits for them, and re-layouts: 7.3 us -> 4.78 us
    unnamed x18 -> x9, local copies, waits for them, and re-layouts: 6.63 us -> 4.27 us
where the time goes in v2:
time: 60.4 us; the launch traced here: 60.1 us
  Pallas kernels  54.7 us (91%)
  local copies, waits for them, and re-layouts  4.78 us (8%)
  between operations  0.65 us (1%)
    pallas_call x1, Pallas kernels, by_groups(): pl.pallas_call(functools.partial(grouped_kernel, n, reps), out_shape=(jax...  54.7 us
    unnamed x9, local copies, waits for them, and re-layouts  4.27 us

profile of v2, /device:TPU:0, one launch (start us, length us, event | category | flops | bytes accessed | tf_op | source)
XLA Modules:
  0.0 60.1 jit_solution(14517035349616278257)
XLA Ops:
  0.6 54.7 %shard_map.111 = (bf16[128,4096]{1,0:T(8,128)(2,1)}, bf16[128,512]{1,0:T(8,128)(2,1)}, f32[1,1024]{1,0:T(1,128)}, f32[1,128]{1,0:T(1,128)}) custom-call(bf16[128,4096]{1,0:T(8,128)(2,1)} %bitcast.17, bf16[128,512]{1,0:T(8,128)(2,1)} %bitcast.20, bf16[128,512]{1,0:T(8,128)(2,1)} %bitcast.21, bf16[128,4096]{1,0:T(8,128)(2,1)} %bitcast.18, s32[64,128]{1,0:T(8,128)} %bitcast.22, ...), custom_call_target="tpu_custom_call" | custom-call | tf_op jit(solution)/shard_map/pallas_call | solution.py:562
  55.4 0.0 copy-start.2
  55.4 0.7 %copy-done.2 = f32[1,128]{1,0:T(1,128)S(1)} copy-done((f32[1,128]{1,0:T(1,128)S(1)}, f32[1,128]{1,0:T(1,128)}, u32[]{:S(2)}) %copy-start.2) | copy-done | bytes 536
  56.0 0.5 slice_bitcast_fusion
  56.5 0.0 copy-start
  56.5 2.3 %copy.15 = bf16[1,128,4096]{2,1,0:T(8,128)(2,1)} copy(bf16[1,128,4096]{2,1,0:T(8,128)(2,1)} %bitcast.16) | data formatting | bytes 2097152
  58.9 0.0 copy-done
  58.9 0.0 copy-start.1
  58.9 0.7 %copy.16 = bf16[1,128,512]{2,1,0:T(8,128)(2,1)} copy(bf16[1,128,512]{2,1,0:T(8,128)(2,1)S(1)} %bitcast.19) | data formatting | bytes 262144
  59.5 0.0 copy-done.1
  59.5 0.6 copy.17
Async XLA Ops:
  55.4 0.7 %copy-start.2 = (f32[1,128]{1,0:T(1,128)S(1)}, f32[1,128]{1,0:T(1,128)}, u32[]{:S(2)}) copy-start(f32[1,128]{1,0:T(1,128)} %get-tuple-element.11) | copy-start | bytes 1540
  56.5 2.3 %copy-start = (bf16[128,512]{1,0:T(8,128)(2,1)S(1)}, bf16[128,512]{1,0:T(8,128)(2,1)}, u32[]{:S(2)}) copy-start(bf16[128,512]{1,0:T(8,128)(2,1)} %get-tuple-element.9) | copy-start | bytes 393220
  58.9 0.7 %copy-start.1 = (f32[1,1024]{1,0:T(1,128)S(1)}, f32[1,1024]{1,0:T(1,128)}, u32[]{:S(2)}) copy-start(f32[1,1024]{1,0:T(1,128)} %get-tuple-element.10) | copy-start | bytes 12292

commit v3 on v2

--- a/solution.py
+++ b/solution.py
@@ -368,10 +368,20 @@
 
     for d in range(n - 1):
         send(4, d).start()
-    for d in range(n - 1):
-        arrival(1, d).wait_recv()
+    def await_block(a, k):
+        @pl.when(k != me)
+        def _():
+            pltpu.make_async_remote_copy(
+                src_ref=target[a].at[k],
+                dst_ref=target[a].at[k],
+                send_sem=send_sem.at[a, 0],
+                recv_sem=recv_sem.at[a, k],
+                device_id={"seq": k},
+                device_id_type=MESH,
+            ).wait_recv()
 
     def forward(k, _):
+        await_block(1, k)
         ending = ends[k]
         readout = jnp.exp(cols[k])
         block_decay = closing(k)
@@ -396,12 +406,11 @@
 
     lax.fori_loop(0, n, forward, 0)
 
-    for d in range(n - 1):
-        arrival(4, d).wait_recv()
     sums[my_rep] = jnp.zeros(sums.shape[1:], F32)
 
     def middle(i, _):
         k = n - 1 - i
+        await_block(4, k)
         inverse = inv[k]
         readout = jnp.exp(cols[k])
         block_decay = closing(k)

time: 60.4 us -> 59.4 us (0.983)
  Pallas kernels: 54.7 us -> 53.7 us
    pallas_call x1, Pallas kernels: 54.7 us -> 53.7 us  [by_groups(): pl.pallas_call(functools.partial(grouped_kernel, n, reps), out_shape=(jax...]
where the time goes in v3:
time: 59.4 us; the launch traced here: 59.1 us
  Pallas kernels  53.7 us (90%)
  local copies, waits for them, and re-layouts  4.78 us (8%)
  between operations  0.65 us (1%)
    pallas_call x1, Pallas kernels, by_groups(): pl.pallas_call(functools.partial(grouped_kernel, n, reps), out_shape=(jax...  53.7 us
    unnamed x9, local copies, waits for them, and re-layouts  4.27 us

profile of v3, /device:TPU:0, one launch (start us, length us, event | category | flops | bytes accessed | tf_op | source)
XLA Modules:
  0.0 59.1 jit_solution(17642005924067965322)
XLA Ops:
  0.6 53.7 %shard_map.111 = (bf16[128,4096]{1,0:T(8,128)(2,1)}, bf16[128,512]{1,0:T(8,128)(2,1)}, f32[1,1024]{1,0:T(1,128)}, f32[1,128]{1,0:T(1,128)}) custom-call(bf16[128,4096]{1,0:T(8,128)(2,1)} %bitcast.17, bf16[128,512]{1,0:T(8,128)(2,1)} %bitcast.20, bf16[128,512]{1,0:T(8,128)(2,1)} %bitcast.21, bf16[128,4096]{1,0:T(8,128)(2,1)} %bitcast.18, s32[64,128]{1,0:T(8,128)} %bitcast.22, ...), custom_call_target="tpu_custom_call" | custom-call | tf_op jit(solution)/shard_map/pallas_call | solution.py:571
  54.3 0.0 copy-start.2
  54.3 0.7 %copy-done.2 = f32[1,128]{1,0:T(1,128)S(1)} copy-done((f32[1,128]{1,0:T(1,128)S(1)}, f32[1,128]{1,0:T(1,128)}, u32[]{:S(2)}) %copy-start.2) | copy-done | bytes 536
  55.0 0.5 slice_bitcast_fusion
  55.5 0.0 copy-start
  55.5 2.3 %copy.15 = bf16[1,128,4096]{2,1,0:T(8,128)(2,1)} copy(bf16[1,128,4096]{2,1,0:T(8,128)(2,1)} %bitcast.16) | data formatting | bytes 2097152
  57.8 0.0 copy-done
  57.8 0.0 copy-start.1
  57.8 0.7 %copy.16 = bf16[1,128,512]{2,1,0:T(8,128)(2,1)} copy(bf16[1,128,512]{2,1,0:T(8,128)(2,1)S(1)} %bitcast.19) | data formatting | bytes 262144
  58.5 0.0 copy-done.1
  58.5 0.6 %copy.17 = f32[1024]{0:T(1024)} copy(f32[1024]{0:T(1024)S(1)} %bitcast.25) | data formatting | bytes 8192
Async XLA Ops:
  54.3 0.7 %copy-start.2 = (f32[1,128]{1,0:T(1,128)S(1)}, f32[1,128]{1,0:T(1,128)}, u32[]{:S(2)}) copy-start(f32[1,128]{1,0:T(1,128)} %get-tuple-element.11) | copy-start | bytes 1540
  55.5 2.3 %copy-start = (bf16[128,512]{1,0:T(8,128)(2,1)S(1)}, bf16[128,512]{1,0:T(8,128)(2,1)}, u32[]{:S(2)}) copy-start(bf16[128,512]{1,0:T(8,128)(2,1)} %get-tuple-element.9) | copy-start | bytes 393220
  57.8 0.7 %copy-start.1 = (f32[1,1024]{1,0:T(1,128)S(1)}, f32[1,1024]{1,0:T(1,128)}, u32[]{:S(2)}) copy-start(f32[1,1024]{1,0:T(1,128)} %get-tuple-element.10) | copy-start | bytes 12292
